TPU v7x, 768 devices: a whole 4x8x12 slice. The times are simulated.
768 devices in a mesh: space: 24 (over x, z_lo, core), shot: 32 (over z_hi, y).
Axes of the slice: x: 4, y: 8, z: 12 (z_hi: 4, z_lo: 3; z = z_hi * 3 + z_lo), core: 2. Of those that a mesh axis runs over, the one named last changes fastest.
Arguments:
- adjoint: float32 [32, 96, 9, 512], P('shot', 'space'), may hold values from -6 to 6
- checkpoint: bfloat16 [32, 96, 9, 512], P('shot', 'space'), may hold values from -6 to 6
- ckpt_scale: int32 [32, 96, 9], P('shot', 'space'), may hold values from -2 to 2
- lame_first: float32 [96, 512], P('space'), may hold values from 1 to 3
- shear_modulus: float32 [96, 512], P('space'), may hold values from 0.5 to 1.5
- buoyancy: float32 [96, 512], P('space'), may hold values from 0.5 to 2
- stiffness: float32 [3, 8, 8], replicated, may hold values from -2 to 2
- lts_level: int32 [96], P('space'), may hold values from 1 to 4, as said below
- neighbour_patch: int32 [96, 6], P('space'), may hold values from 0 to 95, as said below
- neighbour_face: int32 [96, 6], P('space'), may hold values from 0 to 5, as said below
- face_count: int32 [96], P('space'), may hold values from 1 to 6
Outputs:
- adjoint_prev: float32 [32, 96, 9, 512], P('shot', 'space')
- material_grad: float32 [96, 3, 512], P('space')
Inputs may be any that keep to these rules, and one draw needn't show every extreme that they name: `lts_level`: each patch's substeps are 1 or 4; many more patches take 4 among the lowest-numbered quarter of patches. `neighbour_patch`: every entry differs from its own patch number by 1 to 2, and by exactly 2 in some rows. `neighbour_face`: each row is an ordering of the six faces, so the live entries of a patch name distinct faces.
All inputs are finite; a program needn't handle non-finite values.
Results may differ from a plain program's by a relative error of at most 0.0003.
Values sent between devices are 32-bit elements; how exact they have to be, the bound alone decides.
A program may use at most 32 MiB of HBM per device.

v0:
```python
import jax
import jax.numpy as jnp
from jax import lax
from jax.sharding import PartitionSpec as P

SPLINE_EDGE = 8


penalty = 0.5
coarse_step = 0.2
finest_level = lax.Precision.HIGHEST
forward_forms = ("pvabc,ad->pvdbc", "pvabc,bd->pvadc", "pvabc,cd->pvabd")
transposed_forms = ("pvabc,da->pvdbc", "pvabc,db->pvadc", "pvabc,dc->pvabd")
pair_index = ((0, 5, 4), (5, 1, 3), (4, 3, 2))


def extended(shard, sides, width):
    for axis, dim in sides:
        size, length = (lax.axis_size(axis), shard.shape[dim])
        up = [(i, (i + 1) % size) for i in range(size - 1)]
        down = [(j, i) for i, j in up]
        last = lax.slice_in_dim(shard, length - width, length, axis=dim)
        initial = lax.slice_in_dim(shard, 0, width, axis=dim)
        before = lax.ppermute(last, axis, up)
        after = lax.ppermute(initial, axis, down)
        shard = jnp.concatenate([before, shard, after], axis=dim)
    return shard


def along_dim(stacked, matrix, form):
    patch_grid, count = (stacked.shape[0], stacked.shape[1])
    cube = stacked.reshape(patch_grid, count, SPLINE_EDGE, SPLINE_EDGE, SPLINE_EDGE)
    result = jnp.einsum(form, cube, matrix, precision=finest_level)
    return result.reshape(patch_grid, count, SPLINE_EDGE * SPLINE_EDGE * SPLINE_EDGE)


def face_traces(fields):
    patch_grid = fields.shape[0]
    cube = fields.reshape(patch_grid, 9, SPLINE_EDGE, SPLINE_EDGE, SPLINE_EDGE)
    face_list = [
        cube[:, :, 0],
        cube[:, :, SPLINE_EDGE - 1],
        cube[:, :, :, 0],
        cube[:, :, :, SPLINE_EDGE - 1],
        cube[:, :, :, :, 0],
        cube[:, :, :, :, SPLINE_EDGE - 1],
    ]
    return jnp.stack(
        [face.reshape(patch_grid, 9 * SPLINE_EDGE * SPLINE_EDGE) for face in face_list], axis=1
    )


def face_lift(local_faces, partner, neighbour_face, face_count):
    patch_grid = local_faces.shape[0]
    slot_ids = jnp.arange(6, dtype=jnp.int32)
    indicator_vector = (neighbour_face[:, :, None] == slot_ids[None, None, :]).astype(jnp.float32)
    live_mask = (slot_ids[None, :] < face_count[:, None]).astype(jnp.float32)
    local_match = jnp.einsum("auh,ahd->aud", indicator_vector, local_faces, precision=finest_level)
    jump_flux = penalty * live_mask[:, :, None] * (partner - local_match)
    face_indicator = jnp.einsum(
        "anl,ans->als", indicator_vector, jump_flux, precision=finest_level
    ).reshape(patch_grid, 6, 9, SPLINE_EDGE, SPLINE_EDGE)
    cube = jnp.zeros((patch_grid, 9, SPLINE_EDGE, SPLINE_EDGE, SPLINE_EDGE), jnp.float32)
    cube = cube.at[:, :, 0].add(face_indicator[:, 0])
    cube = cube.at[:, :, SPLINE_EDGE - 1].add(face_indicator[:, 1])
    cube = cube.at[:, :, :, 0].add(face_indicator[:, 2])
    cube = cube.at[:, :, :, SPLINE_EDGE - 1].add(face_indicator[:, 3])
    cube = cube.at[:, :, :, :, 0].add(face_indicator[:, 4])
    cube = cube.at[:, :, :, :, SPLINE_EDGE - 1].add(face_indicator[:, 5])
    return cube.reshape(patch_grid, 9, SPLINE_EDGE * SPLINE_EDGE * SPLINE_EDGE)


def forward_slopes(forward, stiffness):
    slopes = []
    for j in range(3):
        stacked = jnp.stack(
            [
                forward[:, 0],
                forward[:, 1],
                forward[:, 2],
                forward[:, 3 + pair_index[0][j]],
                forward[:, 3 + pair_index[1][j]],
                forward[:, 3 + pair_index[2][j]],
            ],
            axis=1,
        )
        slopes.append(along_dim(stacked, stiffness[j], forward_forms[j]))
    return slopes


def adjoint_rate(adj_state, lame_first, shear_modulus, buoyancy, stiffness):
    stress = adj_state[:, 3:9]
    stress_trace = stress[:, 0] + stress[:, 1] + stress[:, 2]
    scaled_vel = buoyancy[:, None] * adj_state[:, 0:3]
    results = []
    for j in range(3):
        stress_terms = []
        for i in range(3):
            term = 2.0 * shear_modulus * stress[:, pair_index[i][j]]
            if i == j:
                term = term + lame_first * stress_trace
            stress_terms.append(term)
        stacked = jnp.stack(
            stress_terms + [scaled_vel[:, 0], scaled_vel[:, 1], scaled_vel[:, 2]], axis=1
        )
        results.append(along_dim(stacked, stiffness[j], transposed_forms[j]))
    rate_vel = [results[0][:, i] + results[1][:, i] + results[2][:, i] for i in range(3)]
    rate_stress = [
        results[0][:, 3],
        results[1][:, 4],
        results[2][:, 5],
        results[2][:, 4] + results[1][:, 5],
        results[2][:, 3] + results[0][:, 5],
        results[1][:, 3] + results[0][:, 4],
    ]
    return jnp.stack(rate_vel + rate_stress, axis=1)


def gradient_rate(adj_state, slopes):
    stress = adj_state[:, 3:9]
    stress_trace = stress[:, 0] + stress[:, 1] + stress[:, 2]
    divergence = slopes[0][:, 0] + slopes[1][:, 1] + slopes[2][:, 2]
    grad_lame = stress_trace * divergence
    grad_shear = 2.0 * (
        stress[:, 0] * slopes[0][:, 0]
        + stress[:, 1] * slopes[1][:, 1]
        + stress[:, 2] * slopes[2][:, 2]
    )
    grad_shear = grad_shear + stress[:, 3] * (slopes[2][:, 1] + slopes[1][:, 2])
    grad_shear = grad_shear + stress[:, 4] * (slopes[2][:, 0] + slopes[0][:, 2])
    grad_shear = grad_shear + stress[:, 5] * (slopes[1][:, 0] + slopes[0][:, 1])
    grad_buoy = adj_state[:, 0] * (slopes[0][:, 3] + slopes[1][:, 3] + slopes[2][:, 3])
    grad_buoy = grad_buoy + adj_state[:, 1] * (slopes[0][:, 4] + slopes[1][:, 4] + slopes[2][:, 4])
    grad_buoy = grad_buoy + adj_state[:, 2] * (slopes[0][:, 5] + slopes[1][:, 5] + slopes[2][:, 5])
    return jnp.stack([grad_lame, grad_shear, grad_buoy], axis=1)


def reverse_window(
    adj_state,
    lifted,
    forward,
    lame_first,
    shear_modulus,
    buoyancy,
    stiffness,
    lts_level,
    combine_sum,
):
    slopes = forward_slopes(forward, stiffness)
    level_float = lts_level.astype(jnp.float32)
    summed = jnp.zeros((adj_state.shape[0], 3, adj_state.shape[2]), jnp.float32)
    for substep in range(4):
        sub_step = jnp.where(substep < lts_level, coarse_step / level_float, jnp.float32(0.0))[
            :, None, None
        ]
        contrib = sub_step * gradient_rate(adj_state, slopes)
        summed = summed + combine_sum(contrib)
        adj_state = adj_state + sub_step * (
            adjoint_rate(adj_state, lame_first, shear_modulus, buoyancy, stiffness) + lifted
        )
    return (adj_state, summed)


def shards(
    adjoint,
    checkpoint,
    ckpt_scale,
    lame_first,
    shear_modulus,
    buoyancy,
    stiffness,
    lts_level,
    neighbour_patch,
    neighbour_face,
    face_count,
):
    adj_state = adjoint[0]
    patch_grid = adj_state.shape[0]
    forward = (
        checkpoint[0].astype(jnp.float32) * jnp.exp2(ckpt_scale[0].astype(jnp.float32))[:, :, None]
    )
    local_faces = face_traces(adj_state)
    window = extended(local_faces, (("space", 0),), patch_grid)
    first_row = lax.axis_index("space") * patch_grid - patch_grid
    flat_rows = window.reshape(-1, 9 * SPLINE_EDGE * SPLINE_EDGE)
    row_index = (neighbour_patch - first_row) * 6 + jnp.bitwise_xor(neighbour_face, 1)
    partner = flat_rows[row_index]
    lifted = face_lift(local_faces, partner, neighbour_face, face_count)
    new_state, summed = reverse_window(
        adj_state,
        lifted,
        forward,
        lame_first,
        shear_modulus,
        buoyancy,
        stiffness,
        lts_level,
        lambda value: lax.psum(value, "shot"),
    )
    return (new_state[None], summed)


def solution(mesh):
    return jax.shard_map(
        shards,
        mesh=mesh,
        in_specs=(
            P("shot", "space", None, None),
            P("shot", "space", None, None),
            P("shot", "space", None),
            P("space", None),
            P("space", None),
            P("space", None),
            P(),
            P("space"),
            P("space", None),
            P("space", None),
            P("space"),
        ),
        out_specs=(P("shot", "space", None, None), P("space", None, None)),
        check_vma=False,
    )
```

profile of v0, /device:TPU:6, one launch (start us, length us, event | category | flops | bytes accessed | tf_op | source)
XLA Modules:
  0.0 319.8 jit_solution(7495846814077595350)
XLA Ops:
  0.6 1.5 reshape_squeeze.3
  2.2 0.7 fusion.158
  2.9 0.9 fusion.157
  4.4 0.6 constant_dynamic-update-slice_fusion.14
  5.0 0.9 copy.82
  6.0 0.9 copy.83
  7.2 1.7 copy.85
  9.1 1.7 copy.86
  12.2 0.6 constant_dynamic-update-slice_fusion.11
  13.9 1.9 collective-permute-start
  15.9 6.2 %collective-permute-start.1 = (f32[4,6,576]{2,0,1:T(4,128)}, f32[4,6,576]{2,0,1:T(4,128)}, u32[]{:S(2)}, u32[]{:S(2)}) collective-permute-start(f32[4,6,576]{2,0,1:T(4,128)} %constant_dynamic-update-slice_fusion.9), channel_id=1, source_target_pairs={{32,0},{64,32},{96,64},{128,96},{160,128},{192,160},{224,192},{256... | collective-permute-start | bytes 165896 | tf_op jit(solution)/shard_map/ppermute | solution.py:25
  23.7 0.8 convolution_bitcast_fusion.8
  25.5 0.8 fusion.64
  26.9 0.8 convolution_bitcast_fusion.9
  28.5 0.6 constant_dynamic-update-slice_fusion.8
  29.1 0.7 reshape.992
  29.8 0.6 fusion.143
  32.1 1.4 convolution_bitcast_fusion.1
  34.0 1.4 convolution_bitcast_fusion
  35.9 0.8 fusion.112
  36.6 0.6 constant_dynamic-update-slice_fusion.7
  37.2 0.6 constant_dynamic-update-slice_fusion.6
  39.6 0.6 constant_dynamic-update-slice_fusion.2
  41.1 1.0 reshape.984
  42.4 1.0 reshape.986
  43.4 1.0 reshape.988
  44.5 0.9 pad_maximum_fusion.4
  45.5 0.6 gather_fusion
  46.2 1.1 fusion
  47.8 0.8 slice_bitcast_fusion.2
  48.8 14.0 %copy.94 = f32[4,9,8,1,8]{3,2,1,0,4:T(8,128)S(1)} copy(f32[4,9,8,1,8]{4,2,1,0,3:T(8,128)S(1)} %get-tuple-element.101) | data formatting | bytes 18432 | tf_op jit(solution)/shard_map/reshape.199
  62.9 3.0 scatter-add.21
  66.1 3.8 %scatter-add.24 = f32[4,9,8,8,8]{3,2,1,0,4:T(8,128)S(1)} dynamic-update-slice(f32[4,9,8,8,8]{3,2,1,0,4:T(8,128)S(1)} %scatter-add.21, f32[4,9,8,1,8]{3,2,1,0,4:T(8,128)S(1)} %slice_add_fusion.1, s32[]{:T(128)} %constant.174.clone.1, s32[]{:T(128)} %constant.174.clone.1, s32[]{:T(128)} %constant.174.clone.1, s32[]{:T(128)} %constant.174.clone.1, s32[]{:T(128)} %constant.174.clone.1) | dynamic-update-slice | bytes 18436 | tf_op jit(solution)/shard_map/scatter-add | solution.py:66
  70.0 1.8 copy.96
  72.1 23.2 %scatter-add.25 = f32[4,9,8,8,8]{3,2,1,0,4:T(8,128)S(1)} dynamic-update-slice(f32[4,9,8,8,8]{3,2,1,0,4:T(8,128)S(1)} %scatter-add.24, f32[4,9,8,1,8]{3,2,1,0,4:T(8,128)S(1)} %slice_add_fusion, s32[]{:T(128)} %constant.174.clone.1, s32[]{:T(128)} %constant.174.clone.1, s32[]{:T(128)} %constant.174.clone.1, s32[]{:T(128)} %constant.186.clone.1, s32[]{:T(128)} %constant.174.clone.1) | dynamic-update-slice | bytes 18436 | tf_op jit(solution)/shard_map/scatter-add | solution.py:67
  95.3 0.9 fusion.70
  96.2 0.9 fusion.68
  97.2 0.6 copy.97
  97.8 0.6 reshape.973
  99.2 0.9 copy.107
  100.4 0.8 copy.104
  102.2 0.8 convolution_bitcast_fusion.7
  104.6 1.8 convolution_bitcast_fusion.6
  107.3 1.7 fusion.62
  110.6 0.9 copy.122
  111.5 0.6 bitcast_multiply_fusion.8
  112.3 0.8 copy.119
  114.1 1.5 convolution_bitcast_fusion.5
  115.9 1.0 reshape.977
  116.9 0.8 stack.341
  118.6 1.8 convolution_bitcast_fusion.4
  120.6 1.0 reshape.978
  121.6 0.8 stack.344
  122.5 1.8 fusion.60
  125.2 0.7 constant_dynamic-update-slice_fusion.32
  126.7 1.0 copy.130
  127.7 1.3 constant_dynamic-update-slice_fusion.50
  129.1 1.2 reshape.972
  130.5 181.7 %psum.34 = f32[4,3,512]{2,0,1:T(4,128)} all-reduce(f32[4,3,512]{2,0,1:T(4,128)S(1)} %fusion.78), channel_id=1, replica_groups=mesh['space'=24,'shot'=32] {'shot'}, use_global_device_ids=true, to_apply=%region_0.0 | all-reduce | flops 6144 | bytes 49152 | tf_op jit(solution)/shard_map/psum | solution.py:198
  313.0 0.8 convolution_bitcast_fusion.3
  314.9 0.8 convolution_bitcast_fusion.2
  316.6 0.8 fusion.58
  318.0 0.8 constant_dynamic-update-slice_fusion
  318.8 0.7 multiply_add_fusion
  (312 shorter events, 27.7 us)
Async XLA Ops:
  4.2 2.8 copy-start.4
  8.9 13.1 %copy-start.1 = (f32[1,4,9,512]{3,1,2,0:T(4,128)S(1)}, f32[1,4,9,512]{3,1,2,0:T(4,128)}, u32[]{:S(2)}) copy-start(f32[1,4,9,512]{3,1,2,0:T(4,128)} %param.23) | copy-start | bytes 221188
  8.9 13.1 %copy-start.5 = (f32[4,512]{1,0:T(4,128)S(1)}, f32[4,512]{1,0:T(4,128)}, u32[]{:S(2)}) copy-start(f32[4,512]{1,0:T(4,128)} %param.27) | copy-start | bytes 24580
  8.9 13.1 %copy-start.34 = (f32[4,512]{1,0:T(4,128)S(1)}, f32[4,512]{1,0:T(4,128)}, u32[]{:S(2)}) copy-start(f32[4,512]{1,0:T(4,128)} %param.26) | copy-start | bytes 24580
  9.1 13.4 %copy-start.33 = (f32[4,512]{1,0:T(4,128)S(1)}, f32[4,512]{1,0:T(4,128)}, u32[]{:S(2)}) copy-start(f32[4,512]{1,0:T(4,128)} %param.28) | copy-start | bytes 24580
  13.9 30.5 %collective-permute-start = (f32[4,6,576]{2,0,1:T(4,128)}, f32[4,6,576]{2,0,1:T(4,128)}, u32[]{:S(2)}, u32[]{:S(2)}) collective-permute-start(f32[4,6,576]{2,0,1:T(4,128)} %constant_dynamic-update-slice_fusion.9), channel_id=1, source_target_pairs={{0,32},{32,64},{64,96},{96,128},{128,160},{160,192},{192,224},{224... | collective-permute-start | bytes 165896 | tf_op jit(solution)/shard_map/ppermute | solution.py:24
  15.9 28.6 %collective-permute-start.1 = (f32[4,6,576]{2,0,1:T(4,128)}, f32[4,6,576]{2,0,1:T(4,128)}, u32[]{:S(2)}, u32[]{:S(2)}) collective-permute-start(f32[4,6,576]{2,0,1:T(4,128)} %constant_dynamic-update-slice_fusion.9), channel_id=1, source_target_pairs={{32,0},{64,32},{96,64},{128,96},{160,128},{192,160},{224,192},{256... | collective-permute-start | bytes 165896 | tf_op jit(solution)/shard_map/ppermute | solution.py:25
  22.3 0.8 copy-start.55
  22.3 0.9 copy-start.44
  22.7 1.0 copy-start.30
  23.3 1.2 copy-start.25
  25.2 14.4 %copy-start.11 = (f32[4,6,512]{2,0,1:T(4,128)}, f32[4,6,512]{2,0,1:T(4,128)S(1)}, u32[]{:S(2)}) copy-start(f32[4,6,512]{2,0,1:T(4,128)S(1)} %reshape.964) | copy-start | bytes 147460
  27.7 1.4 copy-start.46
  27.7 1.4 copy-start.56
  27.7 2.1 copy-start.59
  27.7 2.8 copy-start.60
  27.7 3.9 %slice-start = ((f32[4,9,512]{2,0,1:T(4,128)}), f32[4,4,512]{2,0,1:T(4,128)S(1)}, s32[]{:S(2)}) async-start(f32[4,9,512]{2,0,1:T(4,128)} %copy-done.25), calls=%async_computation | async-start | bytes 65536 | tf_op jit(solution)/shard_map/slice | solution.py:78
  27.8 3.9 %slice-start.1 = ((f32[4,9,512]{2,0,1:T(4,128)}), f32[4,3,512]{2,0,1:T(4,128)S(1)}, s32[]{:S(2)}) async-start(f32[4,9,512]{2,0,1:T(4,128)} %copy-done.25), calls=%async_computation.1 | async-start | bytes 49152 | tf_op jit(solution)/shard_map/slice | solution.py:78
  28.5 11.7 %copy-start.12 = (f32[4,6,512]{2,0,1:T(4,128)}, f32[4,6,512]{2,0,1:T(4,128)S(1)}, u32[]{:S(2)}) copy-start(f32[4,6,512]{2,0,1:T(4,128)S(1)} %reshape.963) | copy-start | bytes 147460
  30.6 1.1 copy-start.42
  35.4 5.4 %copy-start.54 = (s32[24]{0:T(128)S(1)}, s32[24]{0:T(128)}, u32[]{:S(2)}) copy-start(s32[24]{0:T(128)} %reshape.992) | copy-start | bytes 292
  44.5 1.7 copy-start.47
  47.7 1.0 copy-start
  66.1 3.9 %copy-start.3 = (f32[4,9,8,1,8]{4,2,1,0,3:T(8,128)S(1)}, f32[4,9,8,1,8]{4,2,1,0,3:T(8,128)}, u32[]{:S(2)}) copy-start(f32[4,9,8,1,8]{4,2,1,0,3:T(8,128)} %get-tuple-element.100) | copy-start | bytes 27652
  97.8 0.9 copy-start.2
  97.8 0.9 copy-start.43
  97.8 0.9 copy-start.52
  97.8 1.0 copy-start.35
  99.2 2.9 copy-start.31
  101.3 0.6 copy-start.7
  103.7 21.5 %copy-start.13 = (f32[4,6,512]{2,0,1:T(4,128)}, f32[4,6,512]{2,0,1:T(4,128)S(1)}, u32[]{:S(2)}) copy-start(f32[4,6,512]{2,0,1:T(4,128)S(1)} %reshape.974) | copy-start | bytes 147460
  104.0 0.7 copy-start.9
  107.1 18.0 %copy-start.15 = (f32[4,6,512]{2,0,1:T(4,128)}, f32[4,6,512]{2,0,1:T(4,128)S(1)}, u32[]{:S(2)}) copy-start(f32[4,6,512]{2,0,1:T(4,128)S(1)} %reshape.975) | copy-start | bytes 147460
  107.2 2.8 copy-start.50
  107.2 2.9 copy-start.36
  113.2 0.6 copy-start.8
  115.8 1.9 copy-start.45
  117.9 0.7 copy-start.10
  122.4 2.3 copy-start.17
  122.5 2.3 copy-start.19
  122.5 2.4 copy-start.48
  122.5 2.5 copy-start.26
  122.5 2.5 copy-start.27
  122.5 2.5 copy-start.28
  124.3 1.6 copy-start.37
  124.7 1.1 copy-start.23
  126.5 3.8 %copy-start.49 = (f32[4]{0:T(128)S(1)}, f32[4]{0:T(128)}, u32[]{:S(2)}) copy-start(f32[4]{0:T(128)} %get-tuple-element.153) | copy-start | bytes 52
  126.5 3.8 %copy-start.51 = (f32[4]{0:T(128)S(1)}, f32[4]{0:T(128)}, u32[]{:S(2)}) copy-start(f32[4]{0:T(128)} %get-tuple-element.154) | copy-start | bytes 52
  126.5 3.8 %copy-start.53 = (f32[4]{0:T(128)S(1)}, f32[4]{0:T(128)}, u32[]{:S(2)}) copy-start(f32[4]{0:T(128)} %get-tuple-element.155) | copy-start | bytes 52
  126.5 3.8 %copy-start.57 = (f32[4]{0:T(128)S(1)}, f32[4]{0:T(128)}, u32[]{:S(2)}) copy-start(f32[4]{0:T(128)} %get-tuple-element.84) | copy-start | bytes 52
  126.5 185.6 %copy-start.14 = (f32[4,6,512]{2,0,1:T(4,128)S(1)}, f32[4,6,512]{2,0,1:T(4,128)}, u32[]{:S(2)}) copy-start(f32[4,6,512]{2,0,1:T(4,128)} %copy-done.13) | copy-start | bytes 147460
  126.5 185.6 %copy-start.16 = (f32[4,6,512]{2,0,1:T(4,128)S(1)}, f32[4,6,512]{2,0,1:T(4,128)}, u32[]{:S(2)}) copy-start(f32[4,6,512]{2,0,1:T(4,128)} %copy-done.15) | copy-start | bytes 147460
  126.6 185.6 %copy-start.22 = (f32[4,6,512]{2,0,1:T(4,128)S(1)}, f32[4,6,512]{2,0,1:T(4,128)}, u32[]{:S(2)}) copy-start(f32[4,6,512]{2,0,1:T(4,128)} %copy-done.21) | copy-start | bytes 147460
  129.1 183.9 %copy-start.32 = (f32[3,8,8]{2,1,0:T(8,128)S(1)}, f32[3,8,8]{2,1,0:T(8,128)}, u32[]{:S(2)}) copy-start(f32[3,8,8]{2,1,0:T(8,128)} %param.29) | copy-start | bytes 2308
  130.3 182.7 %copy-start.6 = (f32[4,1,8,8,8]{2,4,3,1,0:T(8,128)S(1)}, f32[4,1,8,8,8]{2,4,3,1,0:T(8,128)}, u32[]{:S(2)}) copy-start(f32[4,1,8,8,8]{2,4,3,1,0:T(8,128)} %copy.130) | copy-start | bytes 24580
  312.2 0.6 copy-start.40
  316.5 1.4 copy-start.18
  316.5 1.4 copy-start.20
  316.5 1.4 copy-start.24
  316.5 1.4 copy-start.38
  316.5 1.5 copy-start.39
  316.5 1.5 copy-start.41
  316.5 2.3 copy-start.29
  316.5 2.3 copy-start.58
  (1 other events, 0.6 us)
where the time goes:
time: 323 us; the launch traced here: 320 us
  blocking collectives  182 us (56%)
  local copies, waits for them, and re-layouts  95.3 us (30%)
  matrix products  18.7 us (6%)
  other arithmetic  13.3 us (4%)
  starting transfers between devices  8.08 us (3%)
    psum x1, blocking collectives, shards(): lax.psum(value, 'shot')  182 us
    scatter-add x1, local copies, waits for them, and re-layouts, face_lift(): cube = cube.at[:, :, :, SPLINE_EDGE - 1].add(face_indicator[:, 3])  23.2 us
    dot_general x15, matrix products, along_dim(): result = jnp.einsum(form, cube, matrix, precision=finest_level)  17.4 us
    another operation x3, local copies, waits for them, and re-layouts  16.6 us
    another operation x60, local copies, waits for them, and re-layouts, adjoint_rate(): jnp.stack(stress_terms + [scaled_vel[:, 0], scaled_vel[:, 1], scaled_vel[...  12.2 us
    reshape x15, local copies, waits for them, and re-layouts, along_dim(): result.reshape(patch_grid, count, SPLINE_EDGE * SPLINE_EDGE * SPLINE_EDGE)  9.19 us
    unnamed x148, local copies, waits for them, and re-layouts  8.38 us
  transfers between devices with their start and end apart: 2, of which 0 were waited for; matrix products, arithmetic and copies ran while one was open for 7% of the time, Pallas kernels for 0%

commit v1 on v0

v1 whole, which is shorter than its diff:
```python
import functools

import jax
import jax.numpy as jnp
from jax import lax
from jax.experimental import pallas as pl
from jax.experimental.pallas import tpu as pltpu
from jax.sharding import PartitionSpec as P

ROWS = 8
LANES = 128
FIELDS = 9
GROUP = 8
PAIR = ((0, 5, 4), (5, 1, 3), (4, 3, 2))
MESH = pl.DeviceIdType.MESH
F32 = jnp.float32
BF16 = jnp.bfloat16


def row_roll(x, shift):
    return pltpu.roll(x, shift % ROWS, 0)


def lane_roll(x, shift):
    return pltpu.roll(x, shift % LANES, 1)


def split_dot(pieces, weights):
    x = jnp.concatenate(pieces, axis=0)
    high = x.astype(BF16)
    low = (x - high.astype(F32)).astype(BF16)
    out = jnp.dot(jnp.concatenate([high, low], axis=1), weights, preferred_element_type=F32)
    out = out[:, :LANES] + out[:, LANES:]
    return [out[ROWS * i : ROWS * (i + 1)] for i in range(len(pieces))]


def along_first(pair, table):
    out = [None, None]
    for t in range(2):
        turned = lane_roll(pair[t], 64)
        for r, base in enumerate((pair[t], turned)):
            swapped = row_roll(base, 4)
            for s, value in enumerate((base, swapped)):
                for u in range(2):
                    term = table[((u * 2 + t) * 2 + r) * 2 + s] * value
                    out[u] = term if out[u] is None else out[u] + term
    return out


def derivatives(groups, table, weights_mid, weights_last):
    first = [along_first(pair, table) for pair in groups[0]]
    results = [first]
    for j, weights in ((1, weights_mid), (2, weights_last)):
        flat = split_dot([tile for pair in groups[j] for tile in pair], weights)
        results.append([[flat[2 * i], flat[2 * i + 1]] for i in range(len(groups[j]))])
    return results


def rate_of(state, lam, mu2, buo, table, weights_mid, weights_last):
    tiles = range(2)
    stress = state[3:]
    scaled = [[mu2[t] * stress[k][t] for t in tiles] for k in range(6)]
    for t in tiles:
        bulk = lam[t] * (stress[0][t] + stress[1][t] + stress[2][t])
        for k in range(3):
            scaled[k][t] = scaled[k][t] + bulk
    moved = [[buo[t] * state[i][t] for t in tiles] for i in range(3)]
    groups = [[scaled[PAIR[i][j]] for i in range(3)] + moved for j in range(3)]
    r = derivatives(groups, table, weights_mid, weights_last)
    out = [[r[0][i][t] + r[1][i][t] + r[2][i][t] for t in tiles] for i in range(3)]
    out += [r[0][3], r[1][4], r[2][5]]
    out.append([r[2][4][t] + r[1][5][t] for t in tiles])
    out.append([r[2][3][t] + r[0][5][t] for t in tiles])
    out.append([r[1][3][t] + r[0][4][t] for t in tiles])
    return out


def kernel(
    n_space,
    n_shot,
    adj_hbm,
    ckpt_hbm,
    scale_hbm,
    lam_hbm,
    mu_hbm,
    buo_hbm,
    stiff_hbm,
    level_hbm,
    npatch_hbm,
    nface_hbm,
    count_hbm,
    out_adj,
    out_grad,
    adj_v,
    ckpt_v,
    ckpt_f,
    lam_v,
    mu_v,
    buo_v,
    scale_s,
    stiff_s,
    level_s,
    npatch_s,
    nface_s,
    count_s,
    state_v,
    sum_v,
    slope_v,
    fwd_v,
    mix_v,
    lift_v,
    coef_v,
    own_v,
    step_v,
    mat_v,
    table_v,
    weight_v,
    send_left,
    send_right,
    from_left,
    from_right,
    grad_v,
    part_v,
    level_part_v,
    total_v,
    result_v,
    in_sem,
    halo_send,
    halo_recv,
    scatter_send,
    scatter_recv,
    cross_send,
    cross_recv,
    gather_send,
    gather_recv,
    out_sem,
):
    n_far = n_shot // GROUP
    space = lax.axis_index("space")
    shot = lax.axis_index("shot")
    far, near = shot // GROUP, lax.rem(shot, GROUP)
    right, left = lax.rem(space + 1, n_space), lax.rem(space + n_space - 1, n_space)
    near_peers = [lax.rem(near + k, GROUP) for k in range(GROUP)]
    far_peers = [lax.rem(far + k, n_far) for k in range(n_far)]

    def at_shot(far_index, near_index):
        return (space, far_index * GROUP + near_index)

    barrier = pltpu.get_barrier_semaphore()
    for device in (
        [(left, shot), (right, shot)]
        + [at_shot(far, near_peers[k]) for k in range(1, GROUP)]
        + [at_shot(far_peers[k], near) for k in range(1, n_far)]
    ):
        pl.semaphore_signal(barrier, inc=1, device_id=device, device_id_type=MESH)

    loads = [
        pltpu.make_async_copy(source, target, in_sem.at[i])
        for i, (source, target) in enumerate(
            (
                (adj_hbm.at[0], adj_v),
                (ckpt_hbm.at[0], ckpt_v),
                (lam_hbm, lam_v),
                (mu_hbm, mu_v),
                (buo_hbm, buo_v),
                (scale_hbm, scale_s),
                (stiff_hbm, stiff_s),
                (level_hbm, level_s),
                (npatch_hbm, npatch_s),
                (nface_hbm, nface_s),
                (count_hbm, count_s),
            )
        )
    ]
    for load in loads:
        load.start()

    row = lax.broadcasted_iota(jnp.int32, (ROWS, LANES), 0)
    lane = lax.broadcasted_iota(jnp.int32, (ROWS, LANES), 1)
    patch = row & 3
    half = row >> 2
    side = lane >> 6
    mid = (lane >> 3) & 7
    last = lane & 7

    def by_patch(values):
        out = jnp.where(patch == 0, values[0], values[1])
        out = jnp.where(patch == 2, values[2], out)
        return jnp.where(patch == 3, values[3], out)

    def by_row(ref, field, t):
        out = None
        for h in range(2):
            for p in range(4):
                start = (2 * h + t) * LANES
                line = jnp.broadcast_to(ref[p, field : field + 1, start : start + LANES], (ROWS, LANES))
                out = line if out is None else jnp.where(row == 4 * h + p, line, out)
        return out

    loads[0].wait()
    for f in range(FIELDS):
        for t in range(2):
            state_v[f, t] = by_row(adj_v, f, t)
    for i in range(5):
        for t in range(2):
            even = state_v[2 * i, t]
            odd = state_v[2 * i + 1, t] if 2 * i + 1 < FIELDS else even
            send_right[i, t] = jnp.where(patch < 2, row_roll(even, -2), odd)
            send_left[i, t] = jnp.where(patch < 2, odd, row_roll(even, 2))

    for load in loads[1:]:
        load.wait()

    first_patch = 4 * space
    here = first_patch + patch
    entries = [
        (
            by_patch([nface_s[p, k] for p in range(4)]),
            by_patch([npatch_s[p, k] for p in range(4)]) - here,
        )
        for k in range(6)
    ]
    live_count = by_patch([count_s[p] for p in range(4)])
    offsets = []
    for f in range(6):
        offset = jnp.zeros((ROWS, LANES), jnp.int32)
        for k in range(6):
            face, distance = entries[k]
            offset = jnp.where((face == f) & (k < live_count), distance, offset)
        offsets.append(offset)
    even_patch = (patch & 1) == 0
    low_patch = patch < 2
    candidates = (
        jnp.where(even_patch, 1, -1),
        jnp.where(low_patch, 2, -2),
        jnp.where(even_patch, -1, 1),
        jnp.where(low_patch, -2, 2),
    )
    zero = jnp.zeros((ROWS, LANES), F32)
    first_low = [(half == 0) & (side == 0), None]
    first_high = [None, (half == 1) & (side == 1)]
    for n, wanted in enumerate(candidates):
        weight = [jnp.where(offsets[f] == wanted, 0.5, 0.0) for f in range(6)]
        coef_v[n, 0] = jnp.where(first_low[0], weight[1], zero)
        coef_v[n, 1] = jnp.where(first_high[1], weight[0], zero)
        coef_v[n, 2] = jnp.where(mid == 7, weight[2], jnp.where(mid == 0, weight[3], zero))
        coef_v[n, 3] = jnp.where(last == 7, weight[4], jnp.where(last == 0, weight[5], zero))
    live = [jnp.where(offsets[f] != 0, 0.5, 0.0) for f in range(6)]
    own_rest = (
        jnp.where(mid == 0, live[2], zero)
        + jnp.where(mid == 7, live[3], zero)
        + jnp.where(last == 0, live[4], zero)
        + jnp.where(last == 7, live[5], zero)
    )
    own_v[0] = own_rest + jnp.where(first_low[0], live[0], zero)
    own_v[1] = own_rest + jnp.where(first_high[1], live[1], zero)

    level = by_patch([level_s[p] for p in range(4)])
    step = 0.2 / level.astype(F32)
    for m in range(4):
        step_v[m] = jnp.where(m < level, step, zero)
    for n, (ref, factor) in enumerate(((lam_v, 1.0), (mu_v, 2.0), (buo_v, 1.0))):
        for t in range(2):
            low = ref[:, t * LANES : (t + 1) * LANES]
            high = ref[:, (2 + t) * LANES : (3 + t) * LANES]
            mat_v[n, t] = jnp.concatenate([low, high], axis=0) * factor
    for kind in range(2):
        for u in range(2):
            for t in range(2):
                for r in range(2):
                    for s in range(2):
                        picks = []
                        for h in range(2):
                            for e in range(2):
                                source = 4 * (h ^ s) + 2 * t + (e ^ r)
                                target = 4 * h + 2 * u + e
                                if kind == 0:
                                    picks.append(stiff_s[0, target, source])
                                else:
                                    picks.append(stiff_s[0, source, target])
                        low = jnp.where(side == 0, picks[0], picks[1])
                        high = jnp.where(side == 0, picks[2], picks[3])
                        table_v[kind, ((u * 2 + t) * 2 + r) * 2 + s] = jnp.where(half == 0, low, high)

    tall = lax.broadcasted_iota(jnp.int32, (LANES, LANES), 0)
    wide = lax.broadcasted_iota(jnp.int32, (LANES, LANES), 1)
    mid_mask = ((tall >> 6) == (wide >> 6)) & ((tall & 7) == (wide & 7))
    last_mask = (tall >> 3) == (wide >> 3)
    for kind in range(2):
        for n in range(2):
            j = n + 1
            place = mid if n == 0 else last
            spread = zero
            for a in range(8):
                line = zero
                for d in range(8):
                    value = stiff_s[j, d, a] if kind == 0 else stiff_s[j, a, d]
                    line = jnp.where(place == d, value, line)
                spread = jnp.where(row == a, line, spread)
            if n == 0:
                square = jnp.concatenate(
                    [jnp.broadcast_to(spread[a : a + 1], (ROWS, LANES)) for a in range(8)] * 2, axis=0
                )
                square = jnp.where(mid_mask, square, 0.0)
            else:
                square = jnp.where(last_mask, jnp.concatenate([spread] * 16, axis=0), 0.0)
            high = square.astype(BF16)
            low = (square - high.astype(F32)).astype(BF16)
            weight_v[kind, n, :LANES, :LANES] = high
            weight_v[kind, n, LANES:, :LANES] = high
            weight_v[kind, n, :LANES, LANES:] = low
            weight_v[kind, n, LANES:, LANES:] = low

    pl.semaphore_wait(barrier, 2 + (GROUP - 1) + (n_far - 1))
    halo = [
        pltpu.make_async_remote_copy(
            src_ref=source,
            dst_ref=target,
            send_sem=halo_send.at[i],
            recv_sem=halo_recv.at[i],
            device_id=(device, shot),
            device_id_type=MESH,
        )
        for i, (source, target, device) in enumerate(
            ((send_right, from_left, right), (send_left, from_right, left))
        )
    ]
    for copy in halo:
        copy.start()

    def get(ref):
        return [[ref[f, t] for t in range(2)] for f in range(FIELDS)]

    def adjoint_rate(state):
        return rate_of(
            state,
            [mat_v[0, t] for t in range(2)],
            [mat_v[1, t] for t in range(2)],
            [mat_v[2, t] for t in range(2)],
            [table_v[0, i] for i in range(16)],
            weight_v[0, 0],
            weight_v[0, 1],
        )

    for f in range(FIELDS):
        for t in range(2):
            x = state_v[f, t]
            back, ahead = row_roll(x, -1), row_roll(x, 1)
            inner = (
                jnp.where(even_patch, back, ahead),
                jnp.where(low_patch, row_roll(x, -2), row_roll(x, 2)),
                jnp.where((patch == 0) | (patch == 3), zero, jnp.where(patch == 1, back, ahead)),
            )
            for axis in range(3):
                slot = t if axis == 0 else axis + 1
                mix_v[axis, f, t] = sum(coef_v[n, slot] * inner[n] for n in range(3))
    start = get(state_v)
    rate = adjoint_rate(start)
    for f in range(FIELDS):
        for t in range(2):
            x = start[f][t]
            sum_v[f, t] = step_v[0] * x
            lift_v[f, t] = -own_v[t] * x
            state_v[f, t] = x + step_v[0] * rate[f][t]

    ckpt_f[...] = ckpt_v[...].astype(F32)
    for f in range(FIELDS):
        power = by_patch([scale_s[0, p, f] for p in range(4)])
        power = lax.shift_left(jnp.ones((ROWS, LANES), jnp.int32), power + 2).astype(F32) * 0.25
        for t in range(2):
            fwd_v[f, t] = by_row(ckpt_f, f, t) * power
    fields = get(fwd_v)
    groups = [fields[:3] + [fields[3 + PAIR[i][j]] for i in range(3)] for j in range(3)]
    d = derivatives(groups, [table_v[1, i] for i in range(16)], weight_v[1, 0], weight_v[1, 1])
    for t in range(2):
        slope_v[0, t] = d[0][0][t] + d[1][1][t] + d[2][2][t]
        slope_v[1, t] = 2.0 * d[0][0][t]
        slope_v[2, t] = 2.0 * d[1][1][t]
        slope_v[3, t] = 2.0 * d[2][2][t]
        slope_v[4, t] = d[2][1][t] + d[1][2][t]
        slope_v[5, t] = d[2][0][t] + d[0][2][t]
        slope_v[6, t] = d[1][0][t] + d[0][1][t]
        for i in range(3):
            slope_v[7 + i, t] = d[0][3 + i][t] + d[1][3 + i][t] + d[2][3 + i][t]

    for copy in halo:
        copy.wait()
    outer_patch = (patch == 0) | (patch == 3)
    for f in range(FIELDS):
        mixed = []
        for t in range(2):
            from_l, from_r = from_left[f // 2, t], from_right[f // 2, t]
            if f % 2 == 0:
                two = jnp.where(low_patch, from_l, from_r)
            else:
                two = jnp.where(low_patch, from_r, from_l)
                two = jnp.where(low_patch, row_roll(two, -2), row_roll(two, 2))
            one = jnp.where(patch == 0, row_roll(two, -1), row_roll(two, 1))
            one = jnp.where(outer_patch, one, zero)
            terms = []
            for axis in range(3):
                slot = t if axis == 0 else axis + 1
                terms.append(mix_v[axis, f, t] + coef_v[3, slot] * two + coef_v[2, slot] * one)
            mixed.append(terms)
        for t in range(2):
            across = row_roll(lane_roll(mixed[1 - t][0], 64), 4)
            y, z = mixed[t][1], mixed[t][2]
            y = jnp.where(mid == 0, lane_roll(y, -56), jnp.where(mid == 7, lane_roll(y, 56), zero))
            z = jnp.where(last == 0, lane_roll(z, -7), jnp.where(last == 7, lane_roll(z, 7), zero))
            lift = lift_v[f, t] + across + y + z
            lift_v[f, t] = lift
            state_v[f, t] = state_v[f, t] + step_v[0] * lift

    def advance(m):
        state = get(state_v)
        rate = adjoint_rate(state)
        for f in range(FIELDS):
            for t in range(2):
                x = state[f][t]
                if m < 3:
                    sum_v[f, t] = sum_v[f, t] + step_v[m] * x
                state_v[f, t] = x + step_v[m] * (rate[f][t] + lift_v[f, t])

    advance(1)
    advance(2)

    for t in range(2):
        a = [sum_v[f, t] + step_v[3] * state_v[f, t] for f in range(FIELDS)]
        rows = (
            (a[3] + a[4] + a[5]) * slope_v[0, t],
            sum(a[3 + k] * slope_v[1 + k, t] for k in range(6)),
            sum(a[i] * slope_v[7 + i, t] for i in range(3)),
        )
        for g, value in enumerate(rows):
            for h in range(2):
                for p in range(4):
                    begin = (2 * h + t) * LANES
                    grad_v[p, g : g + 1, begin : begin + LANES] = value[4 * h + p : 4 * h + p + 1]

    def piece(ref, index):
        return ref.at[index // 2, :, pl.ds(pl.multiple_of(lax.rem(index, 2) * 256, 256), 256)]

    scatter = [
        pltpu.make_async_remote_copy(
            src_ref=piece(grad_v, near_peers[k]),
            dst_ref=part_v.at[k],
            send_sem=scatter_send.at[k],
            recv_sem=scatter_recv.at[k],
            device_id=at_shot(far, near_peers[k]),
            device_id_type=MESH,
        )
        for k in range(1, GROUP)
    ]
    for copy in scatter:
        copy.start()

    advance(3)
    for f in range(FIELDS):
        for t in range(2):
            for h in range(2):
                for p in range(4):
                    begin = (2 * h + t) * LANES
                    r = 4 * h + p
                    result_v[p, f : f + 1, begin : begin + LANES] = state_v[f, t, r : r + 1, :]
    store = pltpu.make_async_copy(result_v, out_adj.at[0], out_sem.at[0])
    store.start()

    for copy in scatter:
        copy.wait_recv()
    mine = grad_v[near // 2, :, pl.ds(pl.multiple_of(lax.rem(near, 2) * 256, 256), 256)]
    for k in range(1, GROUP):
        mine = mine + part_v[k]
    level_part_v[far] = mine
    cross = [
        pltpu.make_async_remote_copy(
            src_ref=level_part_v.at[far],
            dst_ref=level_part_v.at[far],
            send_sem=cross_send.at[k],
            recv_sem=cross_recv.at[k],
            device_id=at_shot(far_peers[k], near),
            device_id_type=MESH,
        )
        for k in range(1, n_far)
    ]
    for copy in cross:
        copy.start()
    for copy in cross:
        copy.wait_recv()
    total = level_part_v[0]
    for k in range(1, n_far):
        total = total + level_part_v[k]
    total_v[...] = total
    gather = [
        pltpu.make_async_remote_copy(
            src_ref=total_v,
            dst_ref=piece(out_grad, near),
            send_sem=gather_send.at[k],
            recv_sem=gather_recv.at[k],
            device_id=at_shot(far, near_peers[k]),
            device_id_type=MESH,
        )
        for k in range(1, GROUP)
    ]
    for copy in gather:
        copy.start()
    keep = pltpu.make_async_copy(total_v, piece(out_grad, near), out_sem.at[1])
    keep.start()
    for copy in scatter + cross:
        copy.wait_send()
    store.wait()
    keep.wait()
    for copy in gather:
        copy.wait()


def shards(n_space, n_shot, *operands):
    adjoint, material = operands[0], operands[3]
    n_patch, n_coef = material.shape
    n_far = n_shot // GROUP
    field = (FIELDS, 2, ROWS, LANES)
    halo = (5, 2, ROWS, LANES)
    dma = pltpu.SemaphoreType.DMA
    return pl.pallas_call(
        functools.partial(kernel, n_space, n_shot),
        out_shape=(
            jax.ShapeDtypeStruct(adjoint.shape, F32),
            jax.ShapeDtypeStruct((n_patch, 3, n_coef), F32),
        ),
        in_specs=[pl.BlockSpec(memory_space=pl.ANY)] * 11,
        out_specs=[pl.BlockSpec(memory_space=pl.ANY)] * 2,
        scratch_shapes=[
            pltpu.VMEM((n_patch, FIELDS, n_coef), F32),
            pltpu.VMEM((n_patch, FIELDS, n_coef), BF16),
            pltpu.VMEM((n_patch, FIELDS, n_coef), F32),
            pltpu.VMEM((n_patch, n_coef), F32),
            pltpu.VMEM((n_patch, n_coef), F32),
            pltpu.VMEM((n_patch, n_coef), F32),
            pltpu.SMEM((1, n_patch, FIELDS), jnp.int32),
            pltpu.SMEM((3, 8, 8), F32),
            pltpu.SMEM((n_patch,), jnp.int32),
            pltpu.SMEM((n_patch, 6), jnp.int32),
            pltpu.SMEM((n_patch, 6), jnp.int32),
            pltpu.SMEM((n_patch,), jnp.int32),
            pltpu.VMEM(field, F32),
            pltpu.VMEM(field, F32),
            pltpu.VMEM((10, 2, ROWS, LANES), F32),
            pltpu.VMEM(field, F32),
            pltpu.VMEM((3,) + field, F32),
            pltpu.VMEM(field, F32),
            pltpu.VMEM((4, 4, ROWS, LANES), F32),
            pltpu.VMEM((2, ROWS, LANES), F32),
            pltpu.VMEM((4, ROWS, LANES), F32),
            pltpu.VMEM((3, 2, ROWS, LANES), F32),
            pltpu.VMEM((2, 16, ROWS, LANES), F32),
            pltpu.VMEM((2, 2, 2 * LANES, 2 * LANES), BF16),
            pltpu.VMEM(halo, F32),
            pltpu.VMEM(halo, F32),
            pltpu.VMEM(halo, F32),
            pltpu.VMEM(halo, F32),
            pltpu.VMEM((n_patch, 3, n_coef), F32),
            pltpu.VMEM((GROUP, 3, 256), F32),
            pltpu.VMEM((n_far, 3, 256), F32),
            pltpu.VMEM((3, 256), F32),
            pltpu.VMEM((n_patch, FIELDS, n_coef), F32),
            dma((11,)),
            dma((2,)),
            dma((2,)),
            dma((GROUP,)),
            dma((GROUP,)),
            dma((n_far,)),
            dma((n_far,)),
            dma((GROUP,)),
            dma((GROUP,)),
            dma((2,)),
        ],
        compiler_params=pltpu.CompilerParams(collective_id=0, has_side_effects=True),
    )(*operands)


def solution(mesh):
    return jax.shard_map(
        functools.partial(shards, mesh.shape["space"], mesh.shape["shot"]),
        mesh=mesh,
        in_specs=(
            P("shot", "space", None, None),
            P("shot", "space", None, None),
            P("shot", "space", None),
            P("space", None),
            P("space", None),
            P("space", None),
            P(),
            P("space"),
            P("space", None),
            P("space", None),
            P("space"),
        ),
        out_specs=(P("shot", "space", None, None), P("space", None, None)),
        check_vma=False,
    )
```

time: 323 us -> 42.2 us (0.13)
  the two profiles are of different devices: /device:TPU:6 before, /device:TPU:8 now
where the time goes in v1:
time: 42.2 us; the launch traced here: 42 us
  Pallas kernels  37 us (88%)
  local copies, waits for them, and re-layouts  4.33 us (10%)
  between operations  0.66 us (2%)
    pallas_call x1, Pallas kernels, shards(): pl.pallas_call(functools.partial(kernel, n_space, n_shot), out_shape=(jax...  37 us
    pallas_call x2, local copies, waits for them, and re-layouts, shards(): pl.pallas_call(functools.partial(kernel, n_space, n_shot), out_shape=(jax...  2.21 us
    unnamed x6, local copies, waits for them, and re-layouts  2.12 us

profile of v1, /device:TPU:8, one launch (start us, length us, event | category | flops | bytes accessed | tf_op | source)
XLA Modules:
  0.0 42.0 jit_solution(17156282531359869166)
XLA Ops:
  0.6 0.0 copy-start
  0.6 1.4 %copy.14.ckpt_hbm = bf16[1,4,9,512]{3,2,1,0:T(8,128)(2,1)} copy(bf16[1,4,9,512]{3,1,2,0:T(4,128)(2,1)} %param.12) | data formatting | bytes 73728 | tf_op args[1]
  2.1 0.0 copy-done
  2.1 0.7 %copy.13.adj_hbm = f32[1,4,9,512]{3,2,1,0:T(8,128)} copy(f32[1,4,9,512]{3,1,2,0:T(4,128)S(1)} %copy-done) | data formatting | bytes 147456 | tf_op args[0]
  2.8 37.0 %shard_map.122 = (f32[1,4,9,512]{3,2,1,0:T(8,128)}, f32[4,3,512]{2,1,0:T(4,128)}) custom-call(f32[1,4,9,512]{3,2,1,0:T(8,128)} %copy.13.adj_hbm, bf16[1,4,9,512]{3,2,1,0:T(8,128)(2,1)} %copy.14.ckpt_hbm, s32[1,4,9]{2,1,0:T(4,128)} %scale_hbm.1, f32[4,512]{1,0:T(4,128)} %lam_hbm.1, f32[4,512]{1,0:T(4,128)} %mu_hbm.1, f32[4,512]{1,0:T(4,128)} %buo_hbm.1, ...), custom_call_target="tpu_custom_call" | custom-call | tf_op jit(solution)/shard_map/pallas_call | solution.py:523
  39.7 0.0 copy-start.1
  39.7 1.6 %copy.15 = f32[1,4,9,512]{3,1,2,0:T(4,128)} copy(f32[1,4,9,512]{3,2,1,0:T(8,128)} %get-tuple-element.2) | data formatting | bytes 147456 | tf_op jit(solution)/shard_map/pallas_call | solution.py:523
  41.3 0.0 copy-done.1
  41.3 0.6 %copy.16 = f32[4,3,512]{2,0,1:T(4,128)} copy(f32[4,3,512]{2,1,0:T(4,128)S(1)} %copy-done.1) | data formatting | bytes 49152 | tf_op jit(solution)/shard_map/pallas_call | solution.py:523
Async XLA Ops:
  0.6 1.5 %copy-start = (f32[1,4,9,512]{3,1,2,0:T(4,128)S(1)}, f32[1,4,9,512]{3,1,2,0:T(4,128)}, u32[]{:S(2)}) copy-start(f32[1,4,9,512]{3,1,2,0:T(4,128)} %param.11) | copy-start | bytes 221188
  39.7 1.6 %copy-start.1 = (f32[4,3,512]{2,1,0:T(4,128)S(1)}, f32[4,3,512]{2,1,0:T(4,128)}, u32[]{:S(2)}) copy-start(f32[4,3,512]{2,1,0:T(4,128)} %get-tuple-element.3) | copy-start | bytes 73732

commit v2 on v1

--- a/solution.py
+++ b/solution.py
@@ -120,19 +120,16 @@
     from_left,
     from_right,
     grad_v,
-    part_v,
-    level_part_v,
-    total_v,
+    near_v,
+    far_v,
     result_v,
     in_sem,
     halo_send,
     halo_recv,
-    scatter_send,
-    scatter_recv,
-    cross_send,
-    cross_recv,
-    gather_send,
-    gather_recv,
+    near_send,
+    near_recv,
+    far_send,
+    far_recv,
     out_sem,
 ):
     n_far = n_shot // GROUP
@@ -188,25 +185,38 @@
         out = jnp.where(patch == 2, values[2], out)
         return jnp.where(patch == 3, values[3], out)
 
-    def by_row(ref, field, t):
-        out = None
-        for h in range(2):
-            for p in range(4):
-                start = (2 * h + t) * LANES
-                line = jnp.broadcast_to(ref[p, field : field + 1, start : start + LANES], (ROWS, LANES))
-                out = line if out is None else jnp.where(row == 4 * h + p, line, out)
-        return out
+    def tile(ref, t):
+        low = ref[:, t * LANES : (t + 1) * LANES]
+        high = ref[:, (2 + t) * LANES : (3 + t) * LANES]
+        return jnp.concatenate([low, high], axis=0)
 
     loads[0].wait()
     for f in range(FIELDS):
         for t in range(2):
-            state_v[f, t] = by_row(adj_v, f, t)
+            state_v[f, t] = tile(adj_v.at[f], t)
     for i in range(5):
         for t in range(2):
             even = state_v[2 * i, t]
             odd = state_v[2 * i + 1, t] if 2 * i + 1 < FIELDS else even
             send_right[i, t] = jnp.where(patch < 2, row_roll(even, -2), odd)
             send_left[i, t] = jnp.where(patch < 2, odd, row_roll(even, 2))
+
+    pl.semaphore_wait(barrier, 2 + (GROUP - 1) + (n_far - 1))
+    halo = [
+        pltpu.make_async_remote_copy(
+            src_ref=source,
+            dst_ref=target,
+            send_sem=halo_send.at[i],
+            recv_sem=halo_recv.at[i],
+            device_id=(device, shot),
+            device_id_type=MESH,
+        )
+        for i, (source, target, device) in enumerate(
+            ((send_right, from_left, right), (send_left, from_right, left))
+        )
+    ]
+    for copy in halo:
+        copy.start()
 
     for load in loads[1:]:
         load.wait()
@@ -261,9 +271,7 @@
         step_v[m] = jnp.where(m < level, step, zero)
     for n, (ref, factor) in enumerate(((lam_v, 1.0), (mu_v, 2.0), (buo_v, 1.0))):
         for t in range(2):
-            low = ref[:, t * LANES : (t + 1) * LANES]
-            high = ref[:, (2 + t) * LANES : (3 + t) * LANES]
-            mat_v[n, t] = jnp.concatenate([low, high], axis=0) * factor
+            mat_v[n, t] = tile(ref, t) * factor
     for kind in range(2):
         for u in range(2):
             for t in range(2):
@@ -311,23 +319,6 @@
             weight_v[kind, n, :LANES, LANES:] = low
             weight_v[kind, n, LANES:, LANES:] = low
 
-    pl.semaphore_wait(barrier, 2 + (GROUP - 1) + (n_far - 1))
-    halo = [
-        pltpu.make_async_remote_copy(
-            src_ref=source,
-            dst_ref=target,
-            send_sem=halo_send.at[i],
-            recv_sem=halo_recv.at[i],
-            device_id=(device, shot),
-            device_id_type=MESH,
-        )
-        for i, (source, target, device) in enumerate(
-            ((send_right, from_left, right), (send_left, from_right, left))
-        )
-    ]
-    for copy in halo:
-        copy.start()
-
     def get(ref):
         return [[ref[f, t] for t in range(2)] for f in range(FIELDS)]
 
@@ -368,7 +359,7 @@
         power = by_patch([scale_s[0, p, f] for p in range(4)])
         power = lax.shift_left(jnp.ones((ROWS, LANES), jnp.int32), power + 2).astype(F32) * 0.25
         for t in range(2):
-            fwd_v[f, t] = by_row(ckpt_f, f, t) * power
+            fwd_v[f, t] = tile(ckpt_f.at[f], t) * power
     fields = get(fwd_v)
     groups = [fields[:3] + [fields[3 + PAIR[i][j]] for i in range(3)] for j in range(3)]
     d = derivatives(groups, [table_v[1, i] for i in range(16)], weight_v[1, 0], weight_v[1, 1])
@@ -431,107 +422,109 @@
             sum(a[3 + k] * slope_v[1 + k, t] for k in range(6)),
             sum(a[i] * slope_v[7 + i, t] for i in range(3)),
         )
-        for g, value in enumerate(rows):
-            for h in range(2):
-                for p in range(4):
-                    begin = (2 * h + t) * LANES
-                    grad_v[p, g : g + 1, begin : begin + LANES] = value[4 * h + p : 4 * h + p + 1]
-
-    def piece(ref, index):
-        return ref.at[index // 2, :, pl.ds(pl.multiple_of(lax.rem(index, 2) * 256, 256), 256)]
-
-    scatter = [
-        pltpu.make_async_remote_copy(
-            src_ref=piece(grad_v, near_peers[k]),
-            dst_ref=part_v.at[k],
-            send_sem=scatter_send.at[k],
-            recv_sem=scatter_recv.at[k],
-            device_id=at_shot(far, near_peers[k]),
-            device_id_type=MESH,
-        )
-        for k in range(1, GROUP)
-    ]
-    for copy in scatter:
-        copy.start()
+        for g in range(3):
+            if t == 0:
+                near_v[0, near, g] = rows[g]
+            else:
+                far_v[0, far, g] = rows[g]
+
+    def share_far(n):
+        copies = [
+            pltpu.make_async_remote_copy(
+                src_ref=far_v.at[n, far],
+                dst_ref=far_v.at[n, far],
+                send_sem=far_send.at[n, k],
+                recv_sem=far_recv.at[n, k],
+                device_id=at_shot(far_peers[k], near),
+                device_id_type=MESH,
+            )
+            for k in sorted(range(1, n_far), key=lambda k: -min(k, n_far - k))
+        ]
+        for copy in copies:
+            copy.start()
+        return copies
+
+    def share_near(n):
+        copies = [
+            pltpu.make_async_remote_copy(
+                src_ref=near_v.at[n, near],
+                dst_ref=near_v.at[n, near],
+                send_sem=near_send.at[n, k],
+                recv_sem=near_recv.at[n, k],
+                device_id=at_shot(far, near_peers[k]),
+                device_id_type=MESH,
+            )
+            for k in sorted(range(1, GROUP), key=lambda k: -min(k, GROUP - k))
+        ]
+        for copy in copies:
+            copy.start()
+        return copies
+
+    def total(ref, n, count, g):
+        out = ref[n, 0, g]
+        for k in range(1, count):
+            out = out + ref[n, k, g]
+        return out
+
+    far_one = share_far(0)
+    near_one = share_near(0)
 
     advance(3)
     for f in range(FIELDS):
         for t in range(2):
             for h in range(2):
-                for p in range(4):
-                    begin = (2 * h + t) * LANES
-                    r = 4 * h + p
-                    result_v[p, f : f + 1, begin : begin + LANES] = state_v[f, t, r : r + 1, :]
+                begin = (2 * h + t) * LANES
+                result_v[f, :, begin : begin + LANES] = state_v[f, t, 4 * h : 4 * h + 4, :]
     store = pltpu.make_async_copy(result_v, out_adj.at[0], out_sem.at[0])
     store.start()
 
-    for copy in scatter:
+    for copy in near_one:
         copy.wait_recv()
-    mine = grad_v[near // 2, :, pl.ds(pl.multiple_of(lax.rem(near, 2) * 256, 256), 256)]
-    for k in range(1, GROUP):
-        mine = mine + part_v[k]
-    level_part_v[far] = mine
-    cross = [
-        pltpu.make_async_remote_copy(
-            src_ref=level_part_v.at[far],
-            dst_ref=level_part_v.at[far],
-            send_sem=cross_send.at[k],
-            recv_sem=cross_recv.at[k],
-            device_id=at_shot(far_peers[k], near),
-            device_id_type=MESH,
-        )
-        for k in range(1, n_far)
-    ]
-    for copy in cross:
-        copy.start()
-    for copy in cross:
+    for g in range(3):
+        far_v[1, far, g] = total(near_v, 0, GROUP, g)
+    far_two = share_far(1)
+    for copy in far_one:
         copy.wait_recv()
-    total = level_part_v[0]
-    for k in range(1, n_far):
-        total = total + level_part_v[k]
-    total_v[...] = total
-    gather = [
-        pltpu.make_async_remote_copy(
-            src_ref=total_v,
-            dst_ref=piece(out_grad, near),
-            send_sem=gather_send.at[k],
-            recv_sem=gather_recv.at[k],
-            device_id=at_shot(far, near_peers[k]),
-            device_id_type=MESH,
-        )
-        for k in range(1, GROUP)
-    ]
-    for copy in gather:
-        copy.start()
-    keep = pltpu.make_async_copy(total_v, piece(out_grad, near), out_sem.at[1])
+    for g in range(3):
+        near_v[1, near, g] = total(far_v, 0, n_far, g)
+    near_two = share_near(1)
+
+    for t, copies, ref, count in ((0, far_two, far_v, n_far), (1, near_two, near_v, GROUP)):
+        for copy in copies:
+            copy.wait_recv()
+        for g in range(3):
+            value = total(ref, 1, count, g)
+            for h in range(2):
+                begin = (2 * h + t) * LANES
+                grad_v[g, :, begin : begin + LANES] = value[4 * h : 4 * h + 4]
+    keep = pltpu.make_async_copy(grad_v, out_grad, out_sem.at[1])
     keep.start()
-    for copy in scatter + cross:
+    for copy in far_one + near_one + far_two + near_two:
         copy.wait_send()
     store.wait()
     keep.wait()
-    for copy in gather:
-        copy.wait()
 
 
 def shards(n_space, n_shot, *operands):
-    adjoint, material = operands[0], operands[3]
+    material = operands[3]
     n_patch, n_coef = material.shape
     n_far = n_shot // GROUP
     field = (FIELDS, 2, ROWS, LANES)
     halo = (5, 2, ROWS, LANES)
     dma = pltpu.SemaphoreType.DMA
-    return pl.pallas_call(
+    adjoint, checkpoint = (x.transpose(0, 2, 1, 3) for x in operands[:2])
+    new_state, grads = pl.pallas_call(
         functools.partial(kernel, n_space, n_shot),
         out_shape=(
-            jax.ShapeDtypeStruct(adjoint.shape, F32),
-            jax.ShapeDtypeStruct((n_patch, 3, n_coef), F32),
+            jax.ShapeDtypeStruct((1, FIELDS, n_patch, n_coef), F32),
+            jax.ShapeDtypeStruct((3, n_patch, n_coef), F32),
         ),
         in_specs=[pl.BlockSpec(memory_space=pl.ANY)] * 11,
         out_specs=[pl.BlockSpec(memory_space=pl.ANY)] * 2,
         scratch_shapes=[
-            pltpu.VMEM((n_patch, FIELDS, n_coef), F32),
-            pltpu.VMEM((n_patch, FIELDS, n_coef), BF16),
-            pltpu.VMEM((n_patch, FIELDS, n_coef), F32),
+            pltpu.VMEM((FIELDS, n_patch, n_coef), F32),
+            pltpu.VMEM((FIELDS, n_patch, n_coef), BF16),
+            pltpu.VMEM((FIELDS, n_patch, n_coef), F32),
             pltpu.VMEM((n_patch, n_coef), F32),
             pltpu.VMEM((n_patch, n_coef), F32),
             pltpu.VMEM((n_patch, n_coef), F32),
@@ -557,24 +550,22 @@
             pltpu.VMEM(halo, F32),
             pltpu.VMEM(halo, F32),
             pltpu.VMEM(halo, F32),
-            pltpu.VMEM((n_patch, 3, n_coef), F32),
-            pltpu.VMEM((GROUP, 3, 256), F32),
-            pltpu.VMEM((n_far, 3, 256), F32),
-            pltpu.VMEM((3, 256), F32),
-            pltpu.VMEM((n_patch, FIELDS, n_coef), F32),
+            pltpu.VMEM((3, n_patch, n_coef), F32),
+            pltpu.VMEM((2, GROUP, 3, ROWS, LANES), F32),
+            pltpu.VMEM((2, n_far, 3, ROWS, LANES), F32),
+            pltpu.VMEM((FIELDS, n_patch, n_coef), F32),
             dma((11,)),
             dma((2,)),
             dma((2,)),
-            dma((GROUP,)),
-            dma((GROUP,)),
-            dma((n_far,)),
-            dma((n_far,)),
-            dma((GROUP,)),
-            dma((GROUP,)),
+            dma((2, GROUP)),
+            dma((2, GROUP)),
+            dma((2, n_far)),
+            dma((2, n_far)),
             dma((2,)),
         ],
         compiler_params=pltpu.CompilerParams(collective_id=0, has_side_effects=True),
-    )(*operands)
+    )(adjoint, checkpoint, *operands[2:])
+    return new_state.transpose(0, 2, 1, 3), grads.transpose(1, 0, 2)
 
 
 def solution(mesh):

time: 42.2 us -> 37 us (0.88)
  Pallas kernels: 37 us -> 34 us
  local copies, waits for them, and re-layouts: 4.33 us -> 2.14 us
    pallas_call x1, Pallas kernels: 37 us -> 34 us  [shards(): pl.pallas_call(functools.partial(kernel, n_space, n_shot), out_shape=(jax...]
    pallas_call x2 -> x0, local copies, waits for them, and re-layouts: 2.21 us -> none  [shards(): pl.pallas_call(functools.partial(kernel, n_space, n_shot), out_shape=(jax...]
    unnamed x6 -> x4, local copies, waits for them, and re-layouts: 2.12 us -> 2.14 us
where the time goes in v2:
time: 37 us; the launch traced here: 36.8 us
  Pallas kernels  34 us (92%)
  local copies, waits for them, and re-layouts  2.14 us (6%)
  between operations  0.65 us (2%)
    pallas_call x1, Pallas kernels, shards(): pl.pallas_call(functools.partial(kernel, n_space, n_shot), out_shape=(jax...  34 us
    unnamed x4, local copies, waits for them, and re-layouts  2.14 us

profile of v2, /device:TPU:8, one launch (start us, length us, event | category | flops | bytes accessed | tf_op | source)
XLA Modules:
  0.0 36.8 jit_solution(17758828789878158678)
XLA Ops:
  0.6 34.0 %shard_map.122 = (f32[1,9,4,512]{3,2,1,0:T(4,128)}, f32[3,4,512]{2,1,0:T(4,128)}) custom-call(f32[1,9,4,512]{3,2,1,0:T(4,128)} %bitcast.4, bf16[1,9,4,512]{3,2,1,0:T(4,128)(2,1)} %bitcast.6, s32[1,4,9]{2,1,0:T(4,128)} %scale_hbm.1, f32[4,512]{1,0:T(4,128)} %lam_hbm.1, f32[4,512]{1,0:T(4,128)} %mu_hbm.1, f32[4,512]{1,0:T(4,128)} %buo_hbm.1, ...), custom_call_target="tpu_custom_call" | custom-call | tf_op jit(solution)/shard_map/pallas_call | solution.py:516
  34.6 0.0 copy-start
  34.6 1.5 %copy.15 = f32[1,4,9,512]{3,1,2,0:T(4,128)} copy(f32[1,4,9,512]{3,1,2,0:T(4,128)} %bitcast.5) | data formatting | bytes 147456
  36.2 0.0 copy-done
  36.2 0.6 %copy.16 = f32[4,3,512]{2,0,1:T(4,128)} copy(f32[4,3,512]{2,0,1:T(4,128)S(1)} %bitcast.7) | data formatting | bytes 49152
Async XLA Ops:
  34.6 1.5 %copy-start = (f32[3,4,512]{2,1,0:T(4,128)S(1)}, f32[3,4,512]{2,1,0:T(4,128)}, u32[]{:S(2)}) copy-start(f32[3,4,512]{2,1,0:T(4,128)} %get-tuple-element.5) | copy-start | bytes 73732

commit v3 on v2

--- a/solution.py
+++ b/solution.py
@@ -119,10 +119,8 @@
     send_right,
     from_left,
     from_right,
-    grad_v,
     near_v,
     far_v,
-    result_v,
     in_sem,
     halo_send,
     halo_recv,
@@ -130,7 +128,6 @@
     near_recv,
     far_send,
     far_recv,
-    out_sem,
 ):
     n_far = n_shot // GROUP
     space = lax.axis_index("space")
@@ -474,9 +471,7 @@
         for t in range(2):
             for h in range(2):
                 begin = (2 * h + t) * LANES
-                result_v[f, :, begin : begin + LANES] = state_v[f, t, 4 * h : 4 * h + 4, :]
-    store = pltpu.make_async_copy(result_v, out_adj.at[0], out_sem.at[0])
-    store.start()
+                out_adj[0, f, :, begin : begin + LANES] = state_v[f, t, 4 * h : 4 * h + 4, :]
 
     for copy in near_one:
         copy.wait_recv()
@@ -496,13 +491,20 @@
             value = total(ref, 1, count, g)
             for h in range(2):
                 begin = (2 * h + t) * LANES
-                grad_v[g, :, begin : begin + LANES] = value[4 * h : 4 * h + 4]
-    keep = pltpu.make_async_copy(grad_v, out_grad, out_sem.at[1])
-    keep.start()
+                out_grad[g, :, begin : begin + LANES] = value[4 * h : 4 * h + 4]
     for copy in far_one + near_one + far_two + near_two:
         copy.wait_send()
-    store.wait()
-    keep.wait()
+
+
+def write_back(state, grads, out_state, out_grads, sem):
+    copies = [
+        pltpu.make_async_copy(source, target, sem.at[i])
+        for i, (source, target) in enumerate(((state, out_state), (grads, out_grads)))
+    ]
+    for copy in copies:
+        copy.start()
+    for copy in copies:
+        copy.wait()
 
 
 def shards(n_space, n_shot, *operands):
@@ -516,11 +518,11 @@
     new_state, grads = pl.pallas_call(
         functools.partial(kernel, n_space, n_shot),
         out_shape=(
-            jax.ShapeDtypeStruct((1, FIELDS, n_patch, n_coef), F32),
-            jax.ShapeDtypeStruct((3, n_patch, n_coef), F32),
+            pltpu.VMEM((1, FIELDS, n_patch, n_coef), F32),
+            pltpu.VMEM((3, n_patch, n_coef), F32),
         ),
         in_specs=[pl.BlockSpec(memory_space=pl.ANY)] * 11,
-        out_specs=[pl.BlockSpec(memory_space=pl.ANY)] * 2,
+        out_specs=[pl.BlockSpec(memory_space=pltpu.VMEM)] * 2,
         scratch_shapes=[
             pltpu.VMEM((FIELDS, n_patch, n_coef), F32),
             pltpu.VMEM((FIELDS, n_patch, n_coef), BF16),
@@ -550,10 +552,8 @@
             pltpu.VMEM(halo, F32),
             pltpu.VMEM(halo, F32),
             pltpu.VMEM(halo, F32),
-            pltpu.VMEM((3, n_patch, n_coef), F32),
             pltpu.VMEM((2, GROUP, 3, ROWS, LANES), F32),
             pltpu.VMEM((2, n_far, 3, ROWS, LANES), F32),
-            pltpu.VMEM((FIELDS, n_patch, n_coef), F32),
             dma((11,)),
             dma((2,)),
             dma((2,)),
@@ -561,10 +561,22 @@
             dma((2, GROUP)),
             dma((2, n_far)),
             dma((2, n_far)),
-            dma((2,)),
         ],
-        compiler_params=pltpu.CompilerParams(collective_id=0, has_side_effects=True),
-    )(adjoint, checkpoint, *operands[2:])
+        compiler_params=pltpu.CompilerParams(
+            collective_id=0, has_side_effects=True, vmem_limit_bytes=16 * 2**20
+        ),
+    )(*(pltpu.with_memory_space_constraint(x, pltpu.HBM) for x in (adjoint, checkpoint, *operands[2:])))
+    new_state, grads = pl.pallas_call(
+        write_back,
+        out_shape=(
+            jax.ShapeDtypeStruct(new_state.shape, F32),
+            jax.ShapeDtypeStruct(grads.shape, F32),
+        ),
+        in_specs=[pl.BlockSpec(memory_space=pl.ANY)] * 2,
+        out_specs=[pl.BlockSpec(memory_space=pl.ANY)] * 2,
+        scratch_shapes=[dma((2,))],
+        compiler_params=pltpu.CompilerParams(vmem_limit_bytes=16 * 2**20),
+    )(new_state, grads)
     return new_state.transpose(0, 2, 1, 3), grads.transpose(1, 0, 2)
 
 

time: 37 us -> 34.9 us (0.943)
  local copies, waits for them, and re-layouts: 2.14 us -> 0 us
    unnamed x4 -> x0, local copies, waits for them, and re-layouts: 2.14 us -> none
    pallas_call x1 -> x2, Pallas kernels: 34 us -> 34.1 us  [the longest x1 33.4 us: shards(): pl.pallas_call(functools.partial(kernel, n_space, n_shot), out_shape=(plt...]
where the time goes in v3:
time: 34.9 us; the launch traced here: 34.7 us
  Pallas kernels  34.1 us (98%)
  between operations  0.64 us (2%)
    pallas_call x1, Pallas kernels, shards(): pl.pallas_call(functools.partial(kernel, n_space, n_shot), out_shape=(plt...  33.4 us

profile of v3, /device:TPU:8, one launch (start us, length us, event | category | flops | bytes accessed | tf_op | source)
XLA Modules:
  0.0 34.7 jit_solution(15030610177713362235)
XLA Ops:
  0.6 33.4 %shard_map.122 = (f32[1,9,4,512]{3,2,1,0:T(4,128)S(1)}, f32[3,4,512]{2,1,0:T(4,128)S(1)}) custom-call(f32[1,9,4,512]{3,2,1,0:T(4,128)} %bitcast.4, bf16[1,9,4,512]{3,2,1,0:T(4,128)(2,1)} %bitcast.5, s32[1,4,9]{2,1,0:T(4,128)} %scale_hbm.1, f32[4,512]{1,0:T(4,128)} %lam_hbm.1, f32[4,512]{1,0:T(4,128)} %mu_hbm.1, f32[4,512]{1,0:T(4,128)} %buo_hbm.1, ...), custom_call_target="tpu_custom_call" | custom-call | tf_op jit(solution)/shard_map/pallas_call | solution.py:518
  34.0 0.7 %shard_map.123 = (f32[1,9,4,512]{3,2,1,0:T(4,128)}, f32[3,4,512]{2,1,0:T(4,128)}) custom-call(f32[1,9,4,512]{3,2,1,0:T(4,128)S(1)} %get-tuple-element.6.state, f32[3,4,512]{2,1,0:T(4,128)S(1)} %get-tuple-element.7.grads), custom_call_target="tpu_custom_call" | custom-call | tf_op jit(solution)/shard_map/pallas_call | solution.py:569

commit v4 on v3

--- a/solution.py
+++ b/solution.py
@@ -128,6 +128,7 @@
     near_recv,
     far_send,
     far_recv,
+    answer,
 ):
     n_far = n_shot // GROUP
     space = lax.axis_index("space")
@@ -141,12 +142,18 @@
         return (space, far_index * GROUP + near_index)
 
     barrier = pltpu.get_barrier_semaphore()
-    for device in (
-        [(left, shot), (right, shot)]
-        + [at_shot(far, near_peers[k]) for k in range(1, GROUP)]
-        + [at_shot(far_peers[k], near) for k in range(1, n_far)]
-    ):
-        pl.semaphore_signal(barrier, inc=1, device_id=device, device_id_type=MESH)
+
+
+    def greet(semaphore, device):
+        pl.semaphore_signal(semaphore, inc=1, device_id=device, device_id_type=MESH)
+
+    inner_left, inner_right = space > 0, space < n_space - 1
+    pl.when(inner_left)(functools.partial(greet, barrier, (left, shot)))
+    pl.when(inner_right)(functools.partial(greet, barrier, (right, shot)))
+    for k in range(1, n_far):
+        pl.when(far + k < n_far)(functools.partial(greet, barrier, at_shot(far_peers[k], near)))
+    for k in range(1, GROUP):
+        greet(barrier, at_shot(far, near_peers[k]))
 
     loads = [
         pltpu.make_async_copy(source, target, in_sem.at[i])
@@ -187,6 +194,14 @@
         high = ref[:, (2 + t) * LANES : (3 + t) * LANES]
         return jnp.concatenate([low, high], axis=0)
 
+    @pl.when(space == 0)
+    def _():
+        from_left[...] = jnp.zeros_like(from_left)
+
+    @pl.when(space == n_space - 1)
+    def _():
+        from_right[...] = jnp.zeros_like(from_right)
+
     loads[0].wait()
     for f in range(FIELDS):
         for t in range(2):
@@ -198,7 +213,8 @@
             send_right[i, t] = jnp.where(patch < 2, row_roll(even, -2), odd)
             send_left[i, t] = jnp.where(patch < 2, odd, row_roll(even, 2))
 
-    pl.semaphore_wait(barrier, 2 + (GROUP - 1) + (n_far - 1))
+    sides = (space + n_space - 1) // n_space + (2 * n_space - 2 - space) // n_space
+    pl.semaphore_wait(barrier, sides + (GROUP - 1) + far)
     halo = [
         pltpu.make_async_remote_copy(
             src_ref=source,
@@ -212,8 +228,10 @@
             ((send_right, from_left, right), (send_left, from_right, left))
         )
     ]
-    for copy in halo:
-        copy.start()
+    pl.when(inner_right)(halo[0].start)
+    pl.when(inner_left)(halo[1].start)
+    for k in range(1, n_far):
+        pl.when(far >= k)(functools.partial(greet, answer, at_shot(far_peers[n_far - k], near)))
 
     for load in loads[1:]:
         load.wait()
@@ -371,8 +389,8 @@
         for i in range(3):
             slope_v[7 + i, t] = d[0][3 + i][t] + d[1][3 + i][t] + d[2][3 + i][t]
 
-    for copy in halo:
-        copy.wait()
+    pl.when(inner_left)(halo[0].wait_recv)
+    pl.when(inner_right)(halo[1].wait_recv)
     outer_patch = (patch == 0) | (patch == 3)
     for f in range(FIELDS):
         mixed = []
@@ -426,6 +444,7 @@
                 far_v[0, far, g] = rows[g]
 
     def share_far(n):
+        order = sorted(range(1, n_far), key=lambda k: -min(k, n_far - k))
         copies = [
             pltpu.make_async_remote_copy(
                 src_ref=far_v.at[n, far],
@@ -435,10 +454,17 @@
                 device_id=at_shot(far_peers[k], near),
                 device_id_type=MESH,
             )
-            for k in sorted(range(1, n_far), key=lambda k: -min(k, n_far - k))
+            for k in order
         ]
-        for copy in copies:
-            copy.start()
+        if n:
+            for copy in copies:
+                copy.start()
+            return copies
+        for k, copy in zip(order, copies):
+            pl.when(far + k >= n_far)(copy.start)
+        pl.when(far < n_far - 1)(lambda: pl.semaphore_wait(answer, n_far - 1 - far))
+        for k, copy in zip(order, copies):
+            pl.when(far + k < n_far)(copy.start)
         return copies
 
     def share_near(n):
@@ -463,8 +489,8 @@
             out = out + ref[n, k, g]
         return out
 
+    near_one = share_near(0)
     far_one = share_far(0)
-    near_one = share_near(0)
 
     advance(3)
     for f in range(FIELDS):
@@ -492,6 +518,8 @@
             for h in range(2):
                 begin = (2 * h + t) * LANES
                 out_grad[g, :, begin : begin + LANES] = value[4 * h : 4 * h + 4]
+    pl.when(inner_right)(halo[0].wait_send)
+    pl.when(inner_left)(halo[1].wait_send)
     for copy in far_one + near_one + far_two + near_two:
         copy.wait_send()
 
@@ -561,6 +589,7 @@
             dma((2, GROUP)),
             dma((2, n_far)),
             dma((2, n_far)),
+            pltpu.SemaphoreType.REGULAR,
         ],
         compiler_params=pltpu.CompilerParams(
             collective_id=0, has_side_effects=True, vmem_limit_bytes=16 * 2**20

time: 34.9 us -> 32.9 us (0.943)
  the two profiles are of different devices: /device:TPU:8 before, /device:TPU:6 now
where the time goes in v4:
time: 32.9 us; the launch traced here: 32.7 us
  Pallas kernels  32 us (97%)
  between operations  0.64 us (2%)
    pallas_call x1, Pallas kernels, shards(): pl.pallas_call(functools.partial(kernel, n_space, n_shot), out_shape=(plt...  31.4 us

profile of v4, /device:TPU:6, one launch (start us, length us, event | category | flops | bytes accessed | tf_op | source)
XLA Modules:
  0.0 32.7 jit_solution(15443497502776249514)
XLA Ops:
  0.6 31.4 %shard_map.122 = (f32[1,9,4,512]{3,2,1,0:T(4,128)S(1)}, f32[3,4,512]{2,1,0:T(4,128)S(1)}) custom-call(f32[1,9,4,512]{3,2,1,0:T(4,128)} %bitcast.4, bf16[1,9,4,512]{3,2,1,0:T(4,128)(2,1)} %bitcast.5, s32[1,4,9]{2,1,0:T(4,128)} %scale_hbm.1, f32[4,512]{1,0:T(4,128)} %lam_hbm.1, f32[4,512]{1,0:T(4,128)} %mu_hbm.1, f32[4,512]{1,0:T(4,128)} %buo_hbm.1, ...), custom_call_target="tpu_custom_call" | custom-call | tf_op jit(solution)/shard_map/pallas_call | solution.py:546
  32.0 0.7 %shard_map.123 = (f32[1,9,4,512]{3,2,1,0:T(4,128)}, f32[3,4,512]{2,1,0:T(4,128)}) custom-call(f32[1,9,4,512]{3,2,1,0:T(4,128)S(1)} %get-tuple-element.6.state, f32[3,4,512]{2,1,0:T(4,128)S(1)} %get-tuple-element.7.grads), custom_call_target="tpu_custom_call" | custom-call | tf_op jit(solution)/shard_map/pallas_call | solution.py:598

commit v5 on v4

--- a/solution.py
+++ b/solution.py
@@ -129,6 +129,7 @@
     far_send,
     far_recv,
     answer,
+    near_answer,
 ):
     n_far = n_shot // GROUP
     space = lax.axis_index("space")
@@ -153,7 +154,7 @@
     for k in range(1, n_far):
         pl.when(far + k < n_far)(functools.partial(greet, barrier, at_shot(far_peers[k], near)))
     for k in range(1, GROUP):
-        greet(barrier, at_shot(far, near_peers[k]))
+        pl.when(near + k < GROUP)(functools.partial(greet, barrier, at_shot(far, near_peers[k])))
 
     loads = [
         pltpu.make_async_copy(source, target, in_sem.at[i])
@@ -214,7 +215,7 @@
             send_left[i, t] = jnp.where(patch < 2, odd, row_roll(even, 2))
 
     sides = (space + n_space - 1) // n_space + (2 * n_space - 2 - space) // n_space
-    pl.semaphore_wait(barrier, sides + (GROUP - 1) + far)
+    pl.semaphore_wait(barrier, sides + near + far)
     halo = [
         pltpu.make_async_remote_copy(
             src_ref=source,
@@ -232,6 +233,8 @@
     pl.when(inner_left)(halo[1].start)
     for k in range(1, n_far):
         pl.when(far >= k)(functools.partial(greet, answer, at_shot(far_peers[n_far - k], near)))
+    for k in range(1, GROUP):
+        pl.when(near >= k)(functools.partial(greet, near_answer, at_shot(far, near_peers[GROUP - k])))
 
     for load in loads[1:]:
         load.wait()
@@ -444,7 +447,7 @@
                 far_v[0, far, g] = rows[g]
 
     def share_far(n):
-        order = sorted(range(1, n_far), key=lambda k: -min(k, n_far - k))
+        order = range(1, n_far)
         copies = [
             pltpu.make_async_remote_copy(
                 src_ref=far_v.at[n, far],
@@ -459,12 +462,6 @@
         if n:
             for copy in copies:
                 copy.start()
-            return copies
-        for k, copy in zip(order, copies):
-            pl.when(far + k >= n_far)(copy.start)
-        pl.when(far < n_far - 1)(lambda: pl.semaphore_wait(answer, n_far - 1 - far))
-        for k, copy in zip(order, copies):
-            pl.when(far + k < n_far)(copy.start)
         return copies
 
     def share_near(n):
@@ -479,8 +476,9 @@
             )
             for k in sorted(range(1, GROUP), key=lambda k: -min(k, GROUP - k))
         ]
-        for copy in copies:
-            copy.start()
+        if n:
+            for copy in copies:
+                copy.start()
         return copies
 
     def total(ref, n, count, g):
@@ -489,8 +487,21 @@
             out = out + ref[n, k, g]
         return out
 
+    far_one = share_far(0)
     near_one = share_near(0)
-    far_one = share_far(0)
+    pl.when(near < GROUP - 1)(lambda: pl.semaphore_wait(near_answer, GROUP - 1 - near))
+    near_one[0].start()
+    for k, copy in enumerate(far_one, 1):
+        pl.when(far + k == n_far)(copy.start)
+    for copy in near_one[1:3]:
+        copy.start()
+    for k, copy in enumerate(far_one, 1):
+        pl.when(far + k > n_far)(copy.start)
+    for copy in near_one[3:]:
+        copy.start()
+    pl.when(far < n_far - 1)(lambda: pl.semaphore_wait(answer, n_far - 1 - far))
+    for k, copy in enumerate(far_one, 1):
+        pl.when(far + k < n_far)(copy.start)
 
     advance(3)
     for f in range(FIELDS):
@@ -510,6 +521,11 @@
         near_v[1, near, g] = total(far_v, 0, n_far, g)
     near_two = share_near(1)
 
+    pl.when(inner_right)(halo[0].wait_send)
+    pl.when(inner_left)(halo[1].wait_send)
+    for copy in far_one + near_one + far_two + near_two:
+        copy.wait_send()
+
     for t, copies, ref, count in ((0, far_two, far_v, n_far), (1, near_two, near_v, GROUP)):
         for copy in copies:
             copy.wait_recv()
@@ -518,10 +534,6 @@
             for h in range(2):
                 begin = (2 * h + t) * LANES
                 out_grad[g, :, begin : begin + LANES] = value[4 * h : 4 * h + 4]
-    pl.when(inner_right)(halo[0].wait_send)
-    pl.when(inner_left)(halo[1].wait_send)
-    for copy in far_one + near_one + far_two + near_two:
-        copy.wait_send()
 
 
 def write_back(state, grads, out_state, out_grads, sem):
@@ -590,6 +602,7 @@
             dma((2, n_far)),
             dma((2, n_far)),
             pltpu.SemaphoreType.REGULAR,
+            pltpu.SemaphoreType.REGULAR,
         ],
         compiler_params=pltpu.CompilerParams(
             collective_id=0, has_side_effects=True, vmem_limit_bytes=16 * 2**20

time: 32.9 us -> 32.8 us (level)
  no operation moved by 1% of the time
where the time goes in v5:
time: 32.8 us; the launch traced here: 32.6 us
  Pallas kernels  32 us (98%)
  between operations  0.64 us (2%)
    pallas_call x1, Pallas kernels, shards(): pl.pallas_call(functools.partial(kernel, n_space, n_shot), out_shape=(plt...  31.3 us

profile of v5, /device:TPU:6, one launch (start us, length us, event | category | flops | bytes accessed | tf_op | source)
XLA Modules:
  0.0 32.6 jit_solution(1868129500431998718)
XLA Ops:
  0.6 31.3 %shard_map.122 = (f32[1,9,4,512]{3,2,1,0:T(4,128)S(1)}, f32[3,4,512]{2,1,0:T(4,128)S(1)}) custom-call(f32[1,9,4,512]{3,2,1,0:T(4,128)} %bitcast.4, bf16[1,9,4,512]{3,2,1,0:T(4,128)(2,1)} %bitcast.5, s32[1,4,9]{2,1,0:T(4,128)} %scale_hbm.1, f32[4,512]{1,0:T(4,128)} %lam_hbm.1, f32[4,512]{1,0:T(4,128)} %mu_hbm.1, f32[4,512]{1,0:T(4,128)} %buo_hbm.1, ...), custom_call_target="tpu_custom_call" | custom-call | tf_op jit(solution)/shard_map/pallas_call | solution.py:558
  32.0 0.7 %shard_map.123 = (f32[1,9,4,512]{3,2,1,0:T(4,128)}, f32[3,4,512]{2,1,0:T(4,128)}) custom-call(f32[1,9,4,512]{3,2,1,0:T(4,128)S(1)} %get-tuple-element.6.state, f32[3,4,512]{2,1,0:T(4,128)S(1)} %get-tuple-element.7.grads), custom_call_target="tpu_custom_call" | custom-call | tf_op jit(solution)/shard_map/pallas_call | solution.py:611

commit v6 on v5

--- a/solution.py
+++ b/solution.py
@@ -135,7 +135,7 @@
     space = lax.axis_index("space")
     shot = lax.axis_index("shot")
     far, near = shot // GROUP, lax.rem(shot, GROUP)
-    right, left = lax.rem(space + 1, n_space), lax.rem(space + n_space - 1, n_space)
+    right, left = space + 1, space - 1
     near_peers = [lax.rem(near + k, GROUP) for k in range(GROUP)]
     far_peers = [lax.rem(far + k, n_far) for k in range(n_far)]
 
@@ -207,12 +207,9 @@
     for f in range(FIELDS):
         for t in range(2):
             state_v[f, t] = tile(adj_v.at[f], t)
-    for i in range(5):
-        for t in range(2):
-            even = state_v[2 * i, t]
-            odd = state_v[2 * i + 1, t] if 2 * i + 1 < FIELDS else even
-            send_right[i, t] = jnp.where(patch < 2, row_roll(even, -2), odd)
-            send_left[i, t] = jnp.where(patch < 2, odd, row_roll(even, 2))
+    for f in range(FIELDS):
+        send_right[f] = jnp.where(patch < 2, row_roll(state_v[f, 0], -2), state_v[f, 1])
+        send_left[f] = jnp.where(patch < 2, state_v[f, 1], row_roll(state_v[f, 0], 2))
 
     sides = (space + n_space - 1) // n_space + (2 * n_space - 2 - space) // n_space
     pl.semaphore_wait(barrier, sides + near + far)
@@ -398,8 +395,8 @@
     for f in range(FIELDS):
         mixed = []
         for t in range(2):
-            from_l, from_r = from_left[f // 2, t], from_right[f // 2, t]
-            if f % 2 == 0:
+            from_l, from_r = from_left[f], from_right[f]
+            if t == 0:
                 two = jnp.where(low_patch, from_l, from_r)
             else:
                 two = jnp.where(low_patch, from_r, from_l)
@@ -539,7 +536,7 @@
 def write_back(state, grads, out_state, out_grads, sem):
     copies = [
         pltpu.make_async_copy(source, target, sem.at[i])
-        for i, (source, target) in enumerate(((state, out_state), (grads, out_grads)))
+        for i, (source, target) in enumerate(((grads, out_grads), (state, out_state)))
     ]
     for copy in copies:
         copy.start()
@@ -552,7 +549,7 @@
     n_patch, n_coef = material.shape
     n_far = n_shot // GROUP
     field = (FIELDS, 2, ROWS, LANES)
-    halo = (5, 2, ROWS, LANES)
+    halo = (FIELDS, ROWS, LANES)
     dma = pltpu.SemaphoreType.DMA
     adjoint, checkpoint = (x.transpose(0, 2, 1, 3) for x in operands[:2])
     new_state, grads = pl.pallas_call(

time: 32.8 us -> 32.7 us (level)
  no operation moved by 1% of the time
where the time goes in v6:
time: 32.7 us; the launch traced here: 32.5 us
  Pallas kernels  31.9 us (98%)
  between operations  0.64 us (2%)
    pallas_call x1, Pallas kernels, shards(): pl.pallas_call(functools.partial(kernel, n_space, n_shot), out_shape=(plt...  31.2 us
    pallas_call x1, Pallas kernels, shards(): pl.pallas_call(write_back, out_shape=(jax.ShapeDtypeStruct(new_state.shap...  0.66 us

profile of v6, /device:TPU:6, one launch (start us, length us, event | category | flops | bytes accessed | tf_op | source)
XLA Modules:
  0.0 32.5 jit_solution(7609897896773240108)
XLA Ops:
  0.6 31.2 %shard_map.122 = (f32[1,9,4,512]{3,2,1,0:T(4,128)S(1)}, f32[3,4,512]{2,1,0:T(4,128)S(1)}) custom-call(f32[1,9,4,512]{3,2,1,0:T(4,128)} %bitcast.4, bf16[1,9,4,512]{3,2,1,0:T(4,128)(2,1)} %bitcast.5, s32[1,4,9]{2,1,0:T(4,128)} %scale_hbm.1, f32[4,512]{1,0:T(4,128)} %lam_hbm.1, f32[4,512]{1,0:T(4,128)} %mu_hbm.1, f32[4,512]{1,0:T(4,128)} %buo_hbm.1, ...), custom_call_target="tpu_custom_call" | custom-call | tf_op jit(solution)/shard_map/pallas_call | solution.py:555
  31.9 0.7 %shard_map.123 = (f32[1,9,4,512]{3,2,1,0:T(4,128)}, f32[3,4,512]{2,1,0:T(4,128)}) custom-call(f32[1,9,4,512]{3,2,1,0:T(4,128)S(1)} %get-tuple-element.6.state, f32[3,4,512]{2,1,0:T(4,128)S(1)} %get-tuple-element.7.grads), custom_call_target="tpu_custom_call" | custom-call | tf_op jit(solution)/shard_map/pallas_call | solution.py:608

commit v7 on v6

--- a/solution.py
+++ b/solution.py
@@ -392,6 +392,8 @@
     pl.when(inner_left)(halo[0].wait_recv)
     pl.when(inner_right)(halo[1].wait_recv)
     outer_patch = (patch == 0) | (patch == 3)
+    state = [[] for _ in range(FIELDS)]
+    total_state = [[] for _ in range(FIELDS)]
     for f in range(FIELDS):
         mixed = []
         for t in range(2):
@@ -415,23 +417,24 @@
             z = jnp.where(last == 0, lane_roll(z, -7), jnp.where(last == 7, lane_roll(z, 7), zero))
             lift = lift_v[f, t] + across + y + z
             lift_v[f, t] = lift
-            state_v[f, t] = state_v[f, t] + step_v[0] * lift
-
-    def advance(m):
-        state = get(state_v)
+            state[f].append(state_v[f, t] + step_v[0] * lift)
+            total_state[f].append(sum_v[f, t] + step_v[1] * state[f][t])
+
+    def advance(m, state):
         rate = adjoint_rate(state)
-        for f in range(FIELDS):
-            for t in range(2):
-                x = state[f][t]
-                if m < 3:
-                    sum_v[f, t] = sum_v[f, t] + step_v[m] * x
-                state_v[f, t] = x + step_v[m] * (rate[f][t] + lift_v[f, t])
-
-    advance(1)
-    advance(2)
+        return [
+            [state[f][t] + step_v[m] * (rate[f][t] + lift_v[f, t]) for t in range(2)]
+            for f in range(FIELDS)
+        ]
+
+    for m in (1, 2):
+        state = advance(m, state)
+        total_state = [
+            [total_state[f][t] + step_v[m + 1] * state[f][t] for t in range(2)] for f in range(FIELDS)
+        ]
 
     for t in range(2):
-        a = [sum_v[f, t] + step_v[3] * state_v[f, t] for f in range(FIELDS)]
+        a = [total_state[f][t] for f in range(FIELDS)]
         rows = (
             (a[3] + a[4] + a[5]) * slope_v[0, t],
             sum(a[3 + k] * slope_v[1 + k, t] for k in range(6)),
@@ -500,12 +503,12 @@
     for k, copy in enumerate(far_one, 1):
         pl.when(far + k < n_far)(copy.start)
 
-    advance(3)
+    state = advance(3, state)
     for f in range(FIELDS):
         for t in range(2):
             for h in range(2):
                 begin = (2 * h + t) * LANES
-                out_adj[0, f, :, begin : begin + LANES] = state_v[f, t, 4 * h : 4 * h + 4, :]
+                out_adj[0, f, :, begin : begin + LANES] = state[f][t][4 * h : 4 * h + 4]
 
     for copy in near_one:
         copy.wait_recv()

time: 32.7 us -> 32.7 us (level)
  no operation moved by 1% of the time
where the time goes in v7:
time: 32.7 us; the launch traced here: 32.5 us
  Pallas kernels  31.9 us (98%)
  between operations  0.64 us (2%)
    pallas_call x1, Pallas kernels, shards(): pl.pallas_call(functools.partial(kernel, n_space, n_shot), out_shape=(plt...  31.2 us
    pallas_call x1, Pallas kernels, shards(): pl.pallas_call(write_back, out_shape=(jax.ShapeDtypeStruct(new_state.shap...  0.66 us

profile of v7, /device:TPU:6, one launch (start us, length us, event | category | flops | bytes accessed | tf_op | source)
XLA Modules:
  0.0 32.5 jit_solution(753842231102246482)
XLA Ops:
  0.6 31.2 %shard_map.122 = (f32[1,9,4,512]{3,2,1,0:T(4,128)S(1)}, f32[3,4,512]{2,1,0:T(4,128)S(1)}) custom-call(f32[1,9,4,512]{3,2,1,0:T(4,128)} %bitcast.4, bf16[1,9,4,512]{3,2,1,0:T(4,128)(2,1)} %bitcast.5, s32[1,4,9]{2,1,0:T(4,128)} %scale_hbm.1, f32[4,512]{1,0:T(4,128)} %lam_hbm.1, f32[4,512]{1,0:T(4,128)} %mu_hbm.1, f32[4,512]{1,0:T(4,128)} %buo_hbm.1, ...), custom_call_target="tpu_custom_call" | custom-call | tf_op jit(solution)/shard_map/pallas_call | solution.py:558
  31.9 0.7 %shard_map.123 = (f32[1,9,4,512]{3,2,1,0:T(4,128)}, f32[3,4,512]{2,1,0:T(4,128)}) custom-call(f32[1,9,4,512]{3,2,1,0:T(4,128)S(1)} %get-tuple-element.6.state, f32[3,4,512]{2,1,0:T(4,128)S(1)} %get-tuple-element.7.grads), custom_call_target="tpu_custom_call" | custom-call | tf_op jit(solution)/shard_map/pallas_call | solution.py:611
